TPU v7x, 32 devices: a whole 2x2x4 slice. The times are simulated.
32 devices in a mesh: groups: 2 (over y), sweep: 8 (over z, x), tile: 2 (over core).
Axes of the slice: x: 2, y: 2, z: 4, core: 2. Of those that a mesh axis runs over, the one named last changes fastest.
Arguments:
- point_feats: bfloat16 [524288, 128], P(('groups', 'sweep', 'tile')), parts along dimension 0, may hold values from -6 to 6
- cotangent: bfloat16 [294912, 128], P(('groups', 'sweep', 'tile')), parts along dimension 0, may hold values from -6 to 6
- send_index: int32 [32, 16, 512], P(('groups', 'sweep', 'tile')), parts along dimension 0, may hold values from 0 to 9215, as said below
- point_slot: int32 [524288], P(('groups', 'sweep', 'tile')), parts along dimension 0, may hold values from 0 to 8191, as said below
- live_count: int32 [32], P(('groups', 'sweep', 'tile')), parts along dimension 0, may hold values from 4096 to 16384
- inner_weight: bfloat16 [128, 128], replicated, may hold values from -0.5 to 0.5
- inner_bias: float32 [128], replicated, may hold values from -4 to 4
- outer_weight: bfloat16 [128, 128], replicated, may hold values from -0.5 to 0.5
- outer_bias: float32 [128], replicated, may hold values from -4 to 4
Outputs:
- point_grads: bfloat16 [524288, 128], P(('groups', 'sweep', 'tile')), parts along dimension 0
- inner_grad: float32 [256, 128], P('groups'), parts along dimension 0
- outer_grad: float32 [256, 128], P('groups'), parts along dimension 0
- ibias_grad: float32 [256], P('groups'), parts along dimension 0
- obias_grad: float32 [256], P('groups'), parts along dimension 0
There are 2 independent parts, one for each index of `groups`. A program takes and returns all parts, laid end to end along the dimension named above; an argument that names none is the same for every part. Nothing has to cross between parts.
Inputs may be any that keep to these rules, and one draw needn't show every extreme that they name: send_index[r, d, j] is one of owner r's own 9216 cells, numbered locally; read as one list of 8192 entries per owner (d slowest), its aligned runs of 128 entries take run w's cells from w * 9216 * 256 // 16384 up to but not including (w + 1) * 9216 * 256 // 16384. point_slot on device d indexes the 8192 rows that d receives, owner by owner; the points of the aligned run b of 256 points of one device take rows from 128 * b up to but not including 128 * b + 128.
All inputs are finite; a program needn't handle non-finite values.
Results may differ from a plain program's by a relative error of at most 0.006.
Values may be sent and summed in bfloat16 or wider, within the bound.
A program may use at most 64 MiB of HBM per device.

v0:
```python
import math

import jax
import jax.numpy as jnp
from jax import lax
from jax.sharding import PartitionSpec as P


def silu_slope(values):
    logistic = jax.nn.sigmoid(values)
    return logistic * (1.0 + values * (1.0 - logistic))


def rows_product(left, right):
    return lax.dot_general(
        left, right, (((0,), (0,)), ((), ())), preferred_element_type=jnp.float32
    )


def local(
    point_feats,
    cotangent,
    send_index,
    point_slot,
    live_count,
    inner_weight,
    inner_bias,
    outer_weight,
    outer_bias,
):
    sweeps = lax.axis_size("sweep")
    tiles = lax.axis_size("tile")
    owners = sweeps * tiles
    tok_rows = point_feats.shape[0]
    per_peer = send_index.shape[2]
    channels = cotangent.shape[1]
    cell_rows = cotangent.shape[0]
    scaling = 1.0 / math.sqrt(tok_rows * owners)
    send_runs = owners * per_peer // 128
    window = cell_rows // send_runs
    send_local = (
        send_index[0].reshape(send_runs, 128)
        - (jnp.arange(send_runs, dtype=jnp.int32) * window)[:, None]
    )
    cell_pick = (
        send_local[:, :, None] == jnp.arange(window, dtype=jnp.int32)[None, None, :]
    ).astype(jnp.bfloat16)
    cell_blocks = cotangent.reshape(send_runs, window, channels)
    outgoing = jnp.einsum(
        "rkc,rcf->rkf", cell_pick, cell_blocks, preferred_element_type=jnp.float32
    )
    outgoing = outgoing.astype(jnp.bfloat16).reshape(owners * per_peer, channels)
    received = lax.all_to_all(outgoing, ("sweep", "tile"), split_axis=0, concat_axis=0, tiled=True)
    pre_inner = jnp.dot(point_feats, inner_weight, preferred_element_type=jnp.float32) + inner_bias
    act_inner = jax.nn.silu(pre_inner).astype(jnp.bfloat16)
    pre_outer = jnp.dot(act_inner, outer_weight, preferred_element_type=jnp.float32) + outer_bias
    point_runs = tok_rows // 256
    row_blocks = received.reshape(point_runs, 128, channels)
    slot_local = (point_slot % 128).reshape(point_runs, 256)
    live_mask = (jnp.arange(tok_rows, dtype=jnp.int32) < live_count[0]).reshape(point_runs, 256)
    point_pick = (
        (slot_local[:, :, None] == jnp.arange(128, dtype=jnp.int32)[None, None, :])
        & live_mask[:, :, None]
    ).astype(jnp.bfloat16)
    act_grad = jnp.einsum(
        "rpk,rkf->rpf", point_pick, row_blocks, preferred_element_type=jnp.float32
    )
    act_grad = act_grad.reshape(tok_rows, channels)
    outer_delta = (act_grad * silu_slope(pre_outer)).astype(jnp.bfloat16)
    outer_term = rows_product(act_inner, outer_delta)
    obias_term = jnp.sum(outer_delta.astype(jnp.float32), axis=0)
    back_inner = jnp.dot(outer_delta, outer_weight.T, preferred_element_type=jnp.float32)
    inner_delta = (back_inner * silu_slope(pre_inner)).astype(jnp.bfloat16)
    inner_term = rows_product(point_feats, inner_delta)
    ibias_term = jnp.sum(inner_delta.astype(jnp.float32), axis=0)
    point_grads = jnp.dot(inner_delta, inner_weight.T, preferred_element_type=jnp.float32).astype(
        jnp.bfloat16
    )
    inner_total, outer_total, ibias_total, obias_total = lax.psum(
        (inner_term, outer_term, ibias_term, obias_term), ("sweep", "tile")
    )
    return (
        point_grads,
        inner_total * scaling,
        outer_total * scaling,
        ibias_total * scaling,
        obias_total * scaling,
    )


def solution(mesh):
    placed = (
        P(("groups", "sweep", "tile"), None),
        P(("groups", "sweep", "tile"), None),
        P(("groups", "sweep", "tile"), None, None),
        P(("groups", "sweep", "tile")),
        P(("groups", "sweep", "tile")),
        P(),
        P(),
        P(),
        P(),
    )
    return jax.shard_map(
        local,
        mesh=mesh,
        in_specs=placed,
        out_specs=(
            P(("groups", "sweep", "tile"), None),
            P("groups", None),
            P("groups", None),
            P("groups"),
            P("groups"),
        ),
        check_vma=False,
    )
```

profile of v0, /device:TPU:0, one launch (start us, length us, event | category | flops | bytes accessed | tf_op | source)
XLA Modules:
  0.0 188.1 jit_solution(1224958861466362348)
XLA Ops:
  7.2 0.0 copy-start
  7.2 0.9 reshape_squeeze.3
  8.1 0.1 broadcast_subtract_fusion
  8.2 0.7 copy-done
  8.9 0.0 copy-start.3
  8.9 0.0 copy-start.4
  8.9 0.0 copy-start.6
  8.9 3.8 %fusion.9 = bf16[64,128,128]{2,1,0:T(8,128)(2,1)} fusion(bf16[64,144,128]{2,1,0:T(8,128)(2,1)S(1)} %bitcast.25, s32[64,128]{1,0:T(8,128)S(1)} %broadcast_subtract_fusion), kind=kOutput, calls=%fused_computation.19 | convolution fusion | flops 304218112 | bytes 4489216 | tf_op jit(solution)/shard_map/rkc,rcf->rkf/dot_general | solution.py:49
  12.6 7.4 %all-to-all-start = ((bf16[16,512,128]{2,1,0:T(8,128)(2,1)}), bf16[16,512,128]{2,1,0:T(8,128)(2,1)}, u32[]{:S(2)}, u32[]{:S(2)}) async-start(bf16[16,512,128]{2,1,0:T(8,128)(2,1)} %bitcast.26), calls=%async_computation | async-start | bytes 4194304 | tf_op jit(solution)/shard_map/all_to_all | solution.py:53
  20.0 0.2 all-reduce.4.cloned.1.call-start
  20.3 0.0 copy-done.3
  21.0 0.0 copy-done.4
  21.0 0.0 copy-done.6
  21.0 9.2 %multiply_convert_fusion = (bf16[16384,128]{1,0:T(8,128)(2,1)}, f32[16384,128]{1,0:T(8,128)}) fusion(f32[128]{0:T(128)S(1)} %copy-done.6, bf16[16384,128]{1,0:T(8,128)(2,1)} %param.9, bf16[128,128]{1,0:T(8,128)(2,1)S(1)} %copy-done.4), kind=kOutput, calls=%fused_computation.9 | convolution fusion | flops 549453824 | bytes 16810496 | tf_op jit(solution)/shard_map/dot_general | solution.py:54
  30.3 30.9 %all-to-all-done = bf16[16,512,128]{2,1,0:T(8,128)(2,1)} async-done(((bf16[16,512,128]{2,1,0:T(8,128)(2,1)}), bf16[16,512,128]{2,1,0:T(8,128)(2,1)}, u32[]{:S(2)}, u32[]{:S(2)}) %all-to-all-start) | async-done | bytes 2097184 | tf_op jit(solution)/shard_map/all_to_all | solution.py:53
  61.2 0.0 copy-start.2
  61.2 0.0 copy-start.5
  61.2 0.0 copy-start.7
  61.2 0.0 slice-start
  61.2 8.5 %fusion.3 = f32[64,256,128]{2,1,0:T(8,128)S(1)} fusion(bf16[64,128,128]{2,1,0:T(8,128)(2,1)} %bitcast.3, s32[64,256]{1,0:T(8,128)S(1)} %eq.30, pred[64,256]{1,0:T(8,128)(4,1)S(1)} %add_compare_fusion), kind=kOutput, calls=%fused_computation.13 | convolution fusion | flops 541065216 | bytes 10567680 | tf_op jit(solution)/shard_map/rpk,rkf->rpf/dot_general | solution.py:65
  69.7 0.0 copy-done.2
  69.7 0.0 copy-done.5
  69.7 0.0 copy-done.7
  69.7 0.0 slice-start.1
  69.7 4.4 %convert_reduce_fusion = (f32[128]{0:T(128)S(1)}, bf16[16384,128]{1,0:T(8,128)(2,1)S(1)}) fusion(f32[128]{0:T(128)S(1)} %copy-done.7, bf16[16384,128]{1,0:T(8,128)(2,1)S(1)} %copy-done.2, bf16[128,128]{1,0:T(8,128)(2,1)S(1)} %copy-done.5, f32[64,256,128]{2,1,0:T(8,128)S(1)} %fusion.3), kind=kOutput, calls=%fused_computation.7 | convolution fusion | flops 562036608 | bytes 16811008 | tf_op jit(solution)/shard_map/dot_general | solution.py:56
  74.1 0.0 slice-done
  74.1 0.0 slice-done.1
  74.1 3.6 %convert_reduce_fusion.1 = (f32[128]{0:T(128)S(1)}, bf16[16384,128]{1,0:T(8,128)(2,1)S(1)}) fusion(f32[16384,128]{1,0:T(8,128)S(1)} %bitcast.28, bf16[16384,128]{1,0:T(8,128)(2,1)S(1)} %get-tuple-element.19, bf16[128,128]{1,0:T(8,128)(2,1)S(1)} %copy-done.5), kind=kOutput, calls=%fused_computation.8 | convolution fusion | flops 559939456 | bytes 16810496 | tf_op jit(solution)/shard_map/dot_general | solution.py:72
  77.8 0.0 copy-start.1
  77.8 3.3 %convolution_convert_fusion = bf16[16384,128]{1,0:T(8,128)(2,1)} fusion(bf16[16384,128]{1,0:T(8,128)(2,1)S(1)} %get-tuple-element.17, bf16[128,128]{1,0:T(8,128)(2,1)S(1)} %copy-done.4), kind=kOutput, calls=%fused_computation.4 | convolution fusion | flops 538968064 | bytes 8421376 | tf_op jit(solution)/shard_map/dot_general | solution.py:76
  81.0 0.0 copy-done.1
  81.1 1.9 %convolution_bitcast_fusion = f32[128,128]{0,1:T(8,128)} fusion(bf16[16384,128]{1,0:T(8,128)(2,1)S(1)} %get-tuple-element.17, bf16[16384,128]{1,0:T(8,128)(2,1)S(1)} %copy-done.1), kind=kOutput, calls=%fused_computation.20 | convolution fusion | flops 536870912 | bytes 8454144 | tf_op jit(solution)/shard_map/dot_general | solution.py:15
  83.0 2.0 %fusion.11 = f32[128,128]{0,1:T(8,128)} fusion(bf16[16384,128]{1,0:T(8,128)(2,1)S(1)} %copy-done.2, bf16[16384,128]{1,0:T(8,128)(2,1)S(1)} %get-tuple-element.19), kind=kOutput, calls=%fused_computation.32 | convolution fusion | flops 536870912 | bytes 8454144 | tf_op jit(solution)/shard_map/dot_general | solution.py:15
  85.0 0.0 all-reduce.4.cloned.1.call-update
  85.0 39.3 %all-reduce = (f32[128]{0:T(128)S(1)}, f32[128]{0:T(128)S(1)}) all-reduce(f32[128]{0:T(128)S(1)} %get-tuple-element.16, f32[128]{0:T(128)S(1)} %get-tuple-element.18), channel_id=1, replica_groups=mesh['groups'=2,'sweep'=8,'tile'=2] {'sweep','tile'}, use_global_device_ids=true, to_apply=%region_3.4 | all-reduce | flops 256 | bytes 2048 | tf_op jit(solution)/shard_map/psum | solution.py:79
  124.3 0.5 broadcast_multiply_fusion.2
  124.8 54.1 %all-reduce.4.cloned.1.call-done = (f32[128,128]{0,1:T(8,128)}, f32[128,128]{0,1:T(8,128)}) async-done(((f32[128,128]{0,1:T(8,128)}, f32[128,128]{0,1:T(8,128)}), (f32[128,128]{0,1:T(8,128)}, f32[128,128]{0,1:T(8,128)})) %all-reduce.4.cloned.1.call-update) | async-done | bytes 131088 | tf_op jit(solution)/shard_map/psum | solution.py:79
  178.9 0.9 broadcast_multiply_fusion
  179.8 0.7 copy.15
  180.5 0.7 copy.16
  (5 shorter events, 0.1 us)
Async XLA Ops:
  7.2 1.7 copy-start
  8.9 11.4 %copy-start.3 = (s32[16384]{0:T(1024)S(1)}, s32[16384]{0:T(1024)}, u32[]{:S(2)}) copy-start(s32[16384]{0:T(1024)} %param.12) | copy-start | bytes 196612
  8.9 12.2 %copy-start.4 = (bf16[128,128]{1,0:T(8,128)(2,1)S(1)}, bf16[128,128]{1,0:T(8,128)(2,1)}, u32[]{:S(2)}) copy-start(bf16[128,128]{1,0:T(8,128)(2,1)} %param.14) | copy-start | bytes 98308
  8.9 12.2 %copy-start.6 = (f32[128]{0:T(128)S(1)}, f32[128]{0:T(128)}, u32[]{:S(2)}) copy-start(f32[128]{0:T(128)} %param.15) | copy-start | bytes 1540
  12.6 48.6 %all-to-all-start = ((bf16[16,512,128]{2,1,0:T(8,128)(2,1)}), bf16[16,512,128]{2,1,0:T(8,128)(2,1)}, u32[]{:S(2)}, u32[]{:S(2)}) async-start(bf16[16,512,128]{2,1,0:T(8,128)(2,1)} %bitcast.26), calls=%async_computation | async-start | bytes 4194304 | tf_op jit(solution)/shard_map/all_to_all | solution.py:53
  20.0 158.9 %all-reduce.4.cloned.1.call-start = ((), (), s32[]{:S(2)}) async-start(), calls=%async_computation.1 | async-start | bytes 262144 | tf_op jit(solution)/shard_map/psum | solution.py:79
  61.2 8.5 %copy-start.2 = (bf16[16384,128]{1,0:T(8,128)(2,1)S(1)}, bf16[16384,128]{1,0:T(8,128)(2,1)}, u32[]{:S(2)}) copy-start(bf16[16384,128]{1,0:T(8,128)(2,1)} %get-tuple-element.14) | copy-start | bytes 12582916
  61.2 8.5 %copy-start.5 = (bf16[128,128]{1,0:T(8,128)(2,1)S(1)}, bf16[128,128]{1,0:T(8,128)(2,1)}, u32[]{:S(2)}) copy-start(bf16[128,128]{1,0:T(8,128)(2,1)} %param.16) | copy-start | bytes 98308
  61.2 8.5 %copy-start.7 = (f32[128]{0:T(128)S(1)}, f32[128]{0:T(128)}, u32[]{:S(2)}) copy-start(f32[128]{0:T(128)} %param.17) | copy-start | bytes 1540
  61.2 12.9 %slice-start = ((s8[8388608]{0:T(1024)(128)(4,1)}), s8[4194304]{0:T(1024)(128)(4,1)S(1)}, s32[]{:S(2)}) async-start(s8[8388608]{0:T(1024)(128)(4,1)} %bitcast.27), calls=%async_computation.2 | async-start | bytes 8388608
  69.7 4.4 %slice-start.1 = ((s8[8388608]{0:T(1024)(128)(4,1)}), s8[4194304]{0:T(1024)(128)(4,1)S(1)}, s32[]{:S(2)}) async-start(s8[8388608]{0:T(1024)(128)(4,1)} %bitcast.27), calls=%async_computation.3 | async-start | bytes 8388608
  77.8 3.3 %copy-start.1 = (bf16[16384,128]{1,0:T(8,128)(2,1)S(1)}, bf16[16384,128]{1,0:T(8,128)(2,1)}, u32[]{:S(2)}) copy-start(bf16[16384,128]{1,0:T(8,128)(2,1)} %param.9) | copy-start | bytes 12582916
Sparse Core Ops, SparseCore 0:
  85.1 93.7 all-reduce.3
where the time goes:
time: 190 us; the launch traced here: 188 us
  waiting for transfers between devices  85 us (45%)
  blocking collectives  39.3 us (21%)
  matrix products  36.7 us (19%)
  between operations  14.8 us (8%)
  starting transfers between devices  7.63 us (4%)
  local copies, waits for them, and re-layouts  3.11 us (2%)
    psum x1, waiting for transfers between devices, local(): lax.psum((inner_term, outer_term, ibias_term, obias_term), ('sweep', 'til...  54.1 us
    psum x1, blocking collectives, local(): lax.psum((inner_term, outer_term, ibias_term, obias_term), ('sweep', 'til...  39.3 us
    all_to_all x1, waiting for transfers between devices, local(): lax.all_to_all(outgoing, ('sweep', 'tile'), split_axis=0, concat_axis=0,...  30.9 us
    dot_general x1, matrix products, local(): jnp.dot(point_feats, inner_weight, preferred_element_type=jnp.float32)  9.22 us
    dot_general x1, matrix products, local(): jnp.einsum('rpk,rkf->rpf', point_pick, row_blocks, preferred_element_type...  8.49 us
    all_to_all x1, starting transfers between devices, local(): lax.all_to_all(outgoing, ('sweep', 'tile'), split_axis=0, concat_axis=0,...  7.41 us
    dot_general x1, matrix products, local(): jnp.dot(act_inner, outer_weight, preferred_element_type=jnp.float32)  4.36 us
    dot_general x2, matrix products, rows_product(): lax.dot_general(left, right, (((0,), (0,)), ((), ())), preferred_element_...  3.95 us
  transfers between devices with their start and end apart: 2, of which 2 were waited for; matrix products, arithmetic and copies ran while one was open for 5% of the time, Pallas kernels for 0%

commit v1 on v0

v1 whole, which is shorter than its diff:
```python
import functools
import math

import jax
import jax.numpy as jnp
from jax import lax
from jax.experimental import pallas as pl
from jax.experimental.pallas import tpu as pltpu
from jax.sharding import PartitionSpec as P

LANES = 128
RUN_POINTS = 256
CHUNK = 512


def transposed_dot(left, right):
    return lax.dot_general(
        left, right, (((0,), (0,)), ((), ())), preferred_element_type=jnp.float32
    )


def dot(left, right):
    return jnp.dot(left, right, preferred_element_type=jnp.float32)


def silu_parts(values):
    gate = 0.5 * jnp.tanh(0.5 * values) + 0.5
    act = values * gate
    return act, gate + act * (1.0 - gate)


def kernel(
    sweeps,
    tiles,
    scaling,
    live_ref,
    cot_ref,
    send_ref,
    slot_ref,
    inner_w_ref,
    inner_b_ref,
    outer_w_ref,
    outer_b_ref,
    feats_hbm,
    grads_hbm,
    inner_out,
    outer_out,
    bias_out,
    feats,
    outgoing,
    received,
    act_ref,
    inner_slope,
    outer_slope,
    picks,
    grads,
    inner_wt,
    outer_wt,
    inner_acc,
    outer_acc,
    bias_acc,
    terms,
    term_slots,
    totals,
    bias_term,
    bias_slots,
    feats_sem,
    grads_sem,
    row_send,
    row_recv,
    term_send,
    term_recv,
    bias_send,
    bias_recv,
    total_send,
    total_recv,
):
    owners = sweeps * tiles
    tok_rows = feats.shape[0]
    per_peer = outgoing.shape[0] // owners
    bits = owners.bit_length() - 1
    unit_peers = max(1, LANES // per_peer)
    unit_rows = unit_peers * per_peer
    unit_runs = unit_rows // LANES
    unit_points = unit_runs * RUN_POINTS
    units = owners // unit_peers
    window = cot_ref.shape[0] // (outgoing.shape[0] // LANES)
    share = terms.shape[1]
    feat = feats.shape[1]
    me = lax.axis_index("sweep") * tiles + lax.axis_index("tile")

    def paired(base, step):
        other = 0
        for bit in range(bits):
            scale = 1 << bit
            other = other + ((base // scale + step // scale) % 2) * scale
        return other

    def device(peer):
        return {"sweep": peer // tiles, "tile": peer % tiles}

    def far_near(turn):
        return (units - 1) - turn // 2 - (turn % 2) * (units // 2)

    load = pltpu.make_async_copy(feats_hbm, feats, feats_sem)
    load.start()

    barrier = pltpu.get_barrier_semaphore()

    def greet(step, carry):
        pl.semaphore_signal(
            barrier,
            inc=1,
            device_id=device(paired(me, step)),
            device_id_type=pl.DeviceIdType.MESH,
        )
        return carry

    lax.fori_loop(1, owners, greet, 0)

    def select(unit, target):
        for run in range(unit_runs):
            place = unit * unit_runs + run
            cells = send_ref[place] - place * window
            rows = lax.broadcasted_iota(jnp.int32, (window, LANES), 0)
            pick = jnp.where(rows == cells, 1.0, 0.0).astype(jnp.bfloat16)
            source = cot_ref[pl.ds(pl.multiple_of(place * window, 16), window), :]
            target[pl.ds(pl.multiple_of(place * LANES, LANES), LANES), :] = transposed_dot(
                pick, source
            ).astype(jnp.bfloat16)

    def row_copy(step, peer):
        return pltpu.make_async_remote_copy(
            src_ref=outgoing.at[pl.ds(pl.multiple_of(peer * per_peer, per_peer), per_peer)],
            dst_ref=received.at[pl.ds(pl.multiple_of(me * per_peer, per_peer), per_peer)],
            send_sem=row_send.at[step],
            recv_sem=row_recv.at[step],
            device_id=device(peer),
            device_id_type=pl.DeviceIdType.MESH,
        )

    my_unit = me // unit_peers

    def send_unit(turn, carry):
        unit_step = far_near(turn)
        select(paired(my_unit, unit_step), outgoing)
        for sub in range(unit_peers):
            step = unit_step * unit_peers + sub
            row_copy(step, paired(me, step)).start()
        return carry

    pl.semaphore_wait(barrier, owners - 1)
    lax.fori_loop(0, units - 1, send_unit, 0)
    select(my_unit, outgoing)
    own = pl.ds(pl.multiple_of(me * per_peer, per_peer), per_peer)
    received[own, :] = outgoing[own, :]
    for sub in range(1, unit_peers):
        row_copy(sub, paired(me, sub)).start()

    inner_wt[...] = inner_w_ref[...].T
    outer_wt[...] = outer_w_ref[...].T
    inner_acc[...] = jnp.zeros_like(inner_acc)
    outer_acc[...] = jnp.zeros_like(outer_acc)
    bias_acc[...] = jnp.zeros_like(bias_acc)
    live = live_ref[0]
    load.wait()

    def forward(chunk, carry):
        here = pl.ds(pl.multiple_of(chunk * CHUNK, CHUNK), CHUNK)
        act, slope = silu_parts(dot(feats[here, :], inner_w_ref[...]) + inner_b_ref[...])
        inner_slope[here, :] = slope
        act = act.astype(jnp.bfloat16)
        act_ref[here, :] = act
        _, slope = silu_parts(dot(act, outer_w_ref[...]) + outer_b_ref[...])
        outer_slope[here, :] = slope
        for part in range(CHUNK // LANES):
            line = chunk * (CHUNK // LANES) + part
            slots = slot_ref[line] - (line // (RUN_POINTS // LANES)) * LANES
            points = lax.broadcasted_iota(jnp.int32, (1, LANES), 1) + line * LANES
            slots = jnp.where(points < live, slots, -1)
            rows = lax.broadcasted_iota(jnp.int32, (LANES, LANES), 0)
            pick = jnp.where(rows == slots, 1.0, 0.0)
            picks[pl.ds(pl.multiple_of(line * LANES, LANES), LANES), :] = pick.T.astype(
                jnp.bfloat16
            )
        return carry

    lax.fori_loop(0, tok_rows // CHUNK, forward, 0)

    def out_copy(unit):
        place = pl.ds(pl.multiple_of(unit * unit_points, unit_points), unit_points)
        return pltpu.make_async_copy(grads.at[place], grads_hbm.at[place], grads_sem.at[unit])

    def backward(unit):
        outer_term = jnp.zeros(outer_acc.shape, jnp.float32)
        inner_term = jnp.zeros(inner_acc.shape, jnp.float32)
        outer_bias = jnp.zeros((8, LANES), jnp.float32)
        inner_bias = jnp.zeros((8, LANES), jnp.float32)
        for run in range(unit_runs):
            place = unit * unit_runs + run
            here = pl.ds(pl.multiple_of(place * RUN_POINTS, RUN_POINTS), RUN_POINTS)
            rows = received[pl.ds(pl.multiple_of(place * LANES, LANES), LANES), :]
            delta = (dot(picks[here, :], rows) * outer_slope[here, :]).astype(jnp.bfloat16)
            outer_term += transposed_dot(act_ref[here, :], delta)
            outer_bias += jnp.sum(delta.astype(jnp.float32).reshape(-1, 8, LANES), axis=0)
            delta = (dot(delta, outer_wt[...]) * inner_slope[here, :]).astype(jnp.bfloat16)
            inner_term += transposed_dot(feats[here, :], delta)
            inner_bias += jnp.sum(delta.astype(jnp.float32).reshape(-1, 8, LANES), axis=0)
            grads[here, :] = dot(delta, inner_wt[...]).astype(jnp.bfloat16)
        outer_acc[...] += outer_term
        inner_acc[...] += inner_term
        bias_acc[0] += inner_bias
        bias_acc[1] += outer_bias
        out_copy(unit).start()

    def arrived(unit_step, carry):
        for sub in range(unit_peers):
            step = unit_step * unit_peers + sub
            row_copy(step, paired(me, step)).wait_recv()
        backward(paired(my_unit, unit_step))
        return carry

    for sub in range(1, unit_peers):
        row_copy(sub, paired(me, sub)).wait_recv()
    backward(my_unit)
    lax.fori_loop(1, units // 2, arrived, 0)
    lax.fori_loop(0, units - units // 2, lambda turn, c: arrived(units - 1 - turn, c), 0)

    for place in range(owners):
        low = place * share
        if low < feat:
            terms[place] = inner_acc[low : low + share, :]
        else:
            terms[place] = outer_acc[low - feat : low - feat + share, :]
    bias_term[0:1, :] = jnp.sum(bias_acc[0], axis=0, keepdims=True)
    bias_term[1:2, :] = jnp.sum(bias_acc[1], axis=0, keepdims=True)

    def term_copy(step):
        peer = paired(me, step)
        return pltpu.make_async_remote_copy(
            src_ref=terms.at[peer],
            dst_ref=term_slots.at[me],
            send_sem=term_send.at[step],
            recv_sem=term_recv.at[step],
            device_id=device(peer),
            device_id_type=pl.DeviceIdType.MESH,
        )

    def bias_copy(step):
        return pltpu.make_async_remote_copy(
            src_ref=bias_term,
            dst_ref=bias_slots.at[me],
            send_sem=bias_send.at[step],
            recv_sem=bias_recv.at[step],
            device_id=device(paired(me, step)),
            device_id_type=pl.DeviceIdType.MESH,
        )

    def total_copy(step):
        return pltpu.make_async_remote_copy(
            src_ref=totals.at[me],
            dst_ref=totals.at[me],
            send_sem=total_send.at[step],
            recv_sem=total_recv.at[step],
            device_id=device(paired(me, step)),
            device_id_type=pl.DeviceIdType.MESH,
        )

    def each(act, first=1, last=None):
        def body(turn, carry):
            act(owners - turn)
            return carry

        lax.fori_loop(first, owners, body, 0)

    each(lambda step: term_copy(step).start())
    each(lambda step: bias_copy(step).start())
    term_slots[me] = terms[me]
    bias_slots[me] = bias_term[...]
    each(lambda step: term_copy(step).wait_recv())
    totals[me] = jnp.sum(term_slots[...], axis=0) * scaling
    each(lambda step: total_copy(step).start())
    each(lambda step: bias_copy(step).wait_recv())
    bias_out[...] = jnp.sum(bias_slots[...], axis=0) * scaling
    each(lambda step: row_copy(step, paired(me, step)).wait_send())
    each(lambda step: term_copy(step).wait_send())
    each(lambda step: bias_copy(step).wait_send())

    def drain(unit, carry):
        out_copy(unit).wait()
        return carry

    lax.fori_loop(0, units, drain, 0)
    each(lambda step: total_copy(step).wait_recv())
    for place in range(owners):
        low = place * share
        if low < feat:
            inner_out[low : low + share, :] = totals[place]
        else:
            outer_out[low - feat : low - feat + share, :] = totals[place]
    each(lambda step: total_copy(step).wait_send())


def local(
    point_feats,
    cotangent,
    send_index,
    point_slot,
    live_count,
    inner_weight,
    inner_bias,
    outer_weight,
    outer_bias,
):
    sweeps = lax.axis_size("sweep")
    tiles = lax.axis_size("tile")
    owners = sweeps * tiles
    tok_rows, feat = point_feats.shape
    width, channels = outer_weight.shape
    per_peer = send_index.shape[2]
    rows = owners * per_peer
    units = rows // max(per_peer, LANES)
    share = (feat + width) // owners
    scaling = 1.0 / math.sqrt(tok_rows * owners)
    vmem = pl.BlockSpec(memory_space=pltpu.VMEM)
    dma = pltpu.SemaphoreType.DMA
    half, full = jnp.bfloat16, jnp.float32
    flops = 2 * tok_rows * LANES * LANES * 8
    point_grads, inner_total, outer_total, biases = pl.pallas_call(
        functools.partial(kernel, sweeps, tiles, scaling),
        out_shape=(
            jax.ShapeDtypeStruct((tok_rows, feat), half),
            jax.ShapeDtypeStruct((feat, width), full),
            jax.ShapeDtypeStruct((width, channels), full),
            jax.ShapeDtypeStruct((2, width), full),
        ),
        in_specs=[pl.BlockSpec(memory_space=pltpu.SMEM)]
        + [vmem] * 7
        + [pl.BlockSpec(memory_space=pl.ANY)],
        out_specs=(pl.BlockSpec(memory_space=pl.ANY), vmem, vmem, vmem),
        scratch_shapes=[
            pltpu.VMEM((tok_rows, feat), half),
            pltpu.VMEM((rows, channels), half),
            pltpu.VMEM((rows, channels), half),
            pltpu.VMEM((tok_rows, width), half),
            pltpu.VMEM((tok_rows, width), full),
            pltpu.VMEM((tok_rows, channels), full),
            pltpu.VMEM((tok_rows, LANES), half),
            pltpu.VMEM((tok_rows, feat), half),
            pltpu.VMEM((width, feat), half),
            pltpu.VMEM((channels, width), half),
            pltpu.VMEM((feat, width), full),
            pltpu.VMEM((width, channels), full),
            pltpu.VMEM((2, 8, LANES), full),
            pltpu.VMEM((owners, share, LANES), full),
            pltpu.VMEM((owners, share, LANES), full),
            pltpu.VMEM((owners, share, LANES), full),
            pltpu.VMEM((2, LANES), full),
            pltpu.VMEM((owners, 2, LANES), full),
            dma(()),
            dma((units,)),
        ]
        + [dma((owners,))] * 8,
        compiler_params=pltpu.CompilerParams(
            collective_id=0, has_side_effects=True, vmem_limit_bytes=56 * 1024 * 1024
        ),
        cost_estimate=pl.CostEstimate(
            flops=flops, bytes_accessed=12 * 1024 * 1024, transcendentals=2 * tok_rows * LANES
        ),
        name="exchange",
    )(
        live_count,
        cotangent,
        send_index.reshape(-1, 1, LANES),
        point_slot.reshape(-1, 1, LANES),
        inner_weight,
        inner_bias.reshape(1, -1),
        outer_weight,
        outer_bias.reshape(1, -1),
        point_feats,
    )
    return point_grads, inner_total, outer_total, biases[0], biases[1]


def solution(mesh):
    placed = (
        P(("groups", "sweep", "tile"), None),
        P(("groups", "sweep", "tile"), None),
        P(("groups", "sweep", "tile"), None, None),
        P(("groups", "sweep", "tile")),
        P(("groups", "sweep", "tile")),
        P(),
        P(),
        P(),
        P(),
    )
    return jax.shard_map(
        local,
        mesh=mesh,
        in_specs=placed,
        out_specs=(
            P(("groups", "sweep", "tile"), None),
            P("groups", None),
            P("groups", None),
            P("groups"),
            P("groups"),
        ),
        check_vma=False,
    )
```

time: 190 us -> 77.9 us (0.41)
  waiting for transfers between devices: 85 us -> 0 us
  Pallas kernels: 0 us -> 68.6 us
  blocking collectives: 39.3 us -> 0 us
  matrix products: 36.7 us -> 0 us
  between operations: 14.8 us -> 1.29 us
  starting transfers between devices: 7.63 us -> 0 us
  local copies, waits for them, and re-layouts: 3.11 us -> 7.72 us
    pallas_call x0 -> x1, Pallas kernels: none -> 68.6 us  [local(): pl.pallas_call(functools.partial(kernel, sweeps, tiles, scaling), out_sha...]
    psum x1 -> x0, waiting for transfers between devices: 54.1 us -> none  [local(): lax.psum((inner_term, outer_term, ibias_term, obias_term), ('sweep', 'til...]
    psum x1 -> x0, blocking collectives: 39.3 us -> none  [local(): lax.psum((inner_term, outer_term, ibias_term, obias_term), ('sweep', 'til...]
    dot_general x8 -> x0, matrix products: 36.7 us -> none  [the longest x1 9.22 us: local(): jnp.dot(point_feats, inner_weight, preferred_element_type=jnp.float32)]
    all_to_all x1 -> x0, waiting for transfers between devices: 30.9 us -> none  [local(): lax.all_to_all(outgoing, ('sweep', 'tile'), split_axis=0, concat_axis=0,...]
    all_to_all x1 -> x0, starting transfers between devices: 7.41 us -> none  [local(): lax.all_to_all(outgoing, ('sweep', 'tile'), split_axis=0, concat_axis=0,...]
    unnamed x22 -> x7, local copies, waits for them, and re-layouts: 2.18 us -> 5.04 us
  transfers between devices with their start and end apart: 2 -> 0, of which waited for: 2 -> 0; matrix products, arithmetic and copies ran while one was open for 5% -> 0% of each run, Pallas kernels for 0% -> 0%
where the time goes in v1:
time: 77.9 us; the launch traced here: 77.6 us
  Pallas kernels  68.6 us (88%)
  local copies, waits for them, and re-layouts  7.72 us (10%)
  between operations  1.29 us (2%)
    pallas_call x1, Pallas kernels, local(): pl.pallas_call(functools.partial(kernel, sweeps, tiles, scaling), out_sha...  68.6 us
    unnamed x7, local copies, waits for them, and re-layouts  5.04 us

profile of v1, /device:TPU:0, one launch (start us, length us, event | category | flops | bytes accessed | tf_op | source)
XLA Modules:
  0.0 77.6 jit_solution(8561955037974969190)
XLA Ops:
  1.3 1.4 %reshape.22.send_ref = s32[64,1,128]{2,1,0:T(1,128)} reshape(s32[1,16,512]{2,1,0:T(8,128)} %param.11) | data formatting | bytes 65536 | tf_op jit(solution)/shard_map/reshape | solution.py:374
  2.7 68.6 %exchange.1 = (bf16[16384,128]{1,0:T(8,128)(2,1)}, f32[128,128]{1,0:T(8,128)}, f32[128,128]{1,0:T(8,128)}, f32[2,128]{1,0:T(2,128)}) custom-call(s32[1]{0:T(128)S(6)} %copy.17.live_ref, bf16[9216,128]{1,0:T(8,128)(2,1)} %cot_ref.1, s32[64,1,128]{2,1,0:T(1,128)} %reshape.22.send_ref, s32[128,1,128]{2,1,0:T(1,128)} %bitcast.7, bf16[128,128]{1,0:T(8,128)(2,1)} %inner_w_ref.1, ...), custom_call_target="tpu_custom_call" | custom-call | flops 4294967296 | bytes 12582912 | tf_op jit(solution)/shard_map/exchange/pallas_call | solution.py:329
  71.3 1.3 %slice_bitcast_fusion = (f32[128]{0:T(128)}, f32[128]{0:T(128)}) fusion(f32[2,128]{1,0:T(2,128)} %get-tuple-element.12), kind=kLoop, calls=%fused_computation | loop fusion | bytes 2048 | tf_op jit(solution)/shard_map/squeeze | solution.py:382
  72.6 0.0 copy-start.1
  72.6 0.0 copy-start
  72.6 3.8 %copy.18 = bf16[16384,128]{1,0:T(8,128)(2,1)} copy(bf16[16384,128]{1,0:T(8,128)(2,1)} %get-tuple-element.20) | data formatting | bytes 8388608
  76.4 0.0 copy-done.1
  76.4 0.6 copy.19
  77.0 0.0 copy-done
  77.0 0.6 copy.20
Async XLA Ops:
  72.6 3.8 %copy-start.1 = (f32[128,128]{1,0:T(8,128)S(1)}, f32[128,128]{1,0:T(8,128)}, u32[]{:S(2)}) copy-start(f32[128,128]{1,0:T(8,128)} %get-tuple-element.21) | copy-start | bytes 196612
  72.6 4.4 %copy-start = (f32[128,128]{1,0:T(8,128)S(1)}, f32[128,128]{1,0:T(8,128)}, u32[]{:S(2)}) copy-start(f32[128,128]{1,0:T(8,128)} %get-tuple-element.22) | copy-start | bytes 196612

commit v2 on v1

--- a/solution.py
+++ b/solution.py
@@ -42,9 +42,8 @@
     outer_w_ref,
     outer_b_ref,
     feats_hbm,
-    grads_hbm,
-    inner_out,
-    outer_out,
+    grads,
+    totals,
     bias_out,
     feats,
     outgoing,
@@ -53,7 +52,6 @@
     inner_slope,
     outer_slope,
     picks,
-    grads,
     inner_wt,
     outer_wt,
     inner_acc,
@@ -61,11 +59,10 @@
     bias_acc,
     terms,
     term_slots,
-    totals,
     bias_term,
     bias_slots,
+    index_rows,
     feats_sem,
-    grads_sem,
     row_send,
     row_recv,
     term_send,
@@ -82,7 +79,6 @@
     unit_peers = max(1, LANES // per_peer)
     unit_rows = unit_peers * per_peer
     unit_runs = unit_rows // LANES
-    unit_points = unit_runs * RUN_POINTS
     units = owners // unit_peers
     window = cot_ref.shape[0] // (outgoing.shape[0] // LANES)
     share = terms.shape[1]
@@ -118,10 +114,18 @@
 
     lax.fori_loop(1, owners, greet, 0)
 
+    for peer in range(owners):
+        for low in range(0, per_peer, LANES):
+            piece = min(per_peer, LANES)
+            at = peer * per_peer + low
+            index_rows[at // LANES, :, at % LANES : at % LANES + piece] = send_ref[
+                0, peer : peer + 1, low : low + piece
+            ]
+
     def select(unit, target):
         for run in range(unit_runs):
             place = unit * unit_runs + run
-            cells = send_ref[place] - place * window
+            cells = index_rows[place] - place * window
             rows = lax.broadcasted_iota(jnp.int32, (window, LANES), 0)
             pick = jnp.where(rows == cells, 1.0, 0.0).astype(jnp.bfloat16)
             source = cot_ref[pl.ds(pl.multiple_of(place * window, 16), window), :]
@@ -186,10 +190,6 @@
         return carry
 
     lax.fori_loop(0, tok_rows // CHUNK, forward, 0)
-
-    def out_copy(unit):
-        place = pl.ds(pl.multiple_of(unit * unit_points, unit_points), unit_points)
-        return pltpu.make_async_copy(grads.at[place], grads_hbm.at[place], grads_sem.at[unit])
 
     def backward(unit):
         outer_term = jnp.zeros(outer_acc.shape, jnp.float32)
@@ -211,7 +211,6 @@
         inner_acc[...] += inner_term
         bias_acc[0] += inner_bias
         bias_acc[1] += outer_bias
-        out_copy(unit).start()
 
     def arrived(unit_step, carry):
         for sub in range(unit_peers):
@@ -286,19 +285,22 @@
     each(lambda step: term_copy(step).wait_send())
     each(lambda step: bias_copy(step).wait_send())
 
-    def drain(unit, carry):
-        out_copy(unit).wait()
-        return carry
-
-    lax.fori_loop(0, units, drain, 0)
     each(lambda step: total_copy(step).wait_recv())
-    for place in range(owners):
-        low = place * share
-        if low < feat:
-            inner_out[low : low + share, :] = totals[place]
-        else:
-            outer_out[low - feat : low - feat + share, :] = totals[place]
     each(lambda step: total_copy(step).wait_send())
+
+
+def finish(
+    grads_in, totals_in, biases_in, grads_out, inner_out, outer_out, ibias_out, obias_out, sems
+):
+    inner_parts = inner_out.shape[0] // totals_in.shape[1]
+    outer_parts = totals_in.shape[0] - inner_parts
+    copy = pltpu.make_async_copy(grads_in, grads_out, sems.at[0])
+    copy.start()
+    inner_out[...] = totals_in[:inner_parts].reshape(inner_out.shape)
+    outer_out[...] = totals_in[inner_parts:].reshape(outer_out.shape)
+    ibias_out[...] = biases_in[0]
+    obias_out[...] = biases_in[1]
+    copy.wait()
 
 
 def local(
@@ -319,25 +321,23 @@
     width, channels = outer_weight.shape
     per_peer = send_index.shape[2]
     rows = owners * per_peer
-    units = rows // max(per_peer, LANES)
     share = (feat + width) // owners
     scaling = 1.0 / math.sqrt(tok_rows * owners)
     vmem = pl.BlockSpec(memory_space=pltpu.VMEM)
     dma = pltpu.SemaphoreType.DMA
     half, full = jnp.bfloat16, jnp.float32
     flops = 2 * tok_rows * LANES * LANES * 8
-    point_grads, inner_total, outer_total, biases = pl.pallas_call(
+    grads, totals, biases = pl.pallas_call(
         functools.partial(kernel, sweeps, tiles, scaling),
         out_shape=(
-            jax.ShapeDtypeStruct((tok_rows, feat), half),
-            jax.ShapeDtypeStruct((feat, width), full),
-            jax.ShapeDtypeStruct((width, channels), full),
-            jax.ShapeDtypeStruct((2, width), full),
+            pltpu.VMEM((tok_rows, feat), half),
+            pltpu.VMEM((owners, share, LANES), full),
+            pltpu.VMEM((2, width), full),
         ),
         in_specs=[pl.BlockSpec(memory_space=pltpu.SMEM)]
         + [vmem] * 7
         + [pl.BlockSpec(memory_space=pl.ANY)],
-        out_specs=(pl.BlockSpec(memory_space=pl.ANY), vmem, vmem, vmem),
+        out_specs=(vmem, vmem, vmem),
         scratch_shapes=[
             pltpu.VMEM((tok_rows, feat), half),
             pltpu.VMEM((rows, channels), half),
@@ -346,7 +346,6 @@
             pltpu.VMEM((tok_rows, width), full),
             pltpu.VMEM((tok_rows, channels), full),
             pltpu.VMEM((tok_rows, LANES), half),
-            pltpu.VMEM((tok_rows, feat), half),
             pltpu.VMEM((width, feat), half),
             pltpu.VMEM((channels, width), half),
             pltpu.VMEM((feat, width), full),
@@ -354,11 +353,10 @@
             pltpu.VMEM((2, 8, LANES), full),
             pltpu.VMEM((owners, share, LANES), full),
             pltpu.VMEM((owners, share, LANES), full),
-            pltpu.VMEM((owners, share, LANES), full),
             pltpu.VMEM((2, LANES), full),
             pltpu.VMEM((owners, 2, LANES), full),
+            pltpu.VMEM((rows // LANES, 1, LANES), jnp.int32),
             dma(()),
-            dma((units,)),
         ]
         + [dma((owners,))] * 8,
         compiler_params=pltpu.CompilerParams(
@@ -371,7 +369,7 @@
     )(
         live_count,
         cotangent,
-        send_index.reshape(-1, 1, LANES),
+        send_index,
         point_slot.reshape(-1, 1, LANES),
         inner_weight,
         inner_bias.reshape(1, -1),
@@ -379,7 +377,20 @@
         outer_bias.reshape(1, -1),
         point_feats,
     )
-    return point_grads, inner_total, outer_total, biases[0], biases[1]
+    return pl.pallas_call(
+        finish,
+        out_shape=(
+            jax.ShapeDtypeStruct((tok_rows, feat), half),
+            jax.ShapeDtypeStruct((feat, width), full),
+            jax.ShapeDtypeStruct((width, channels), full),
+            jax.ShapeDtypeStruct((width,), full),
+            jax.ShapeDtypeStruct((channels,), full),
+        ),
+        in_specs=[vmem, vmem, vmem],
+        out_specs=(pl.BlockSpec(memory_space=pl.ANY), vmem, vmem, vmem, vmem),
+        scratch_shapes=[dma((1,))],
+        name="finish",
+    )(grads, totals, biases)
 
 
 def solution(mesh):

time: 77.9 us -> 77.4 us (level)
  local copies, waits for them, and re-layouts: 7.72 us -> 3.17 us
  Pallas kernels: 68.6 us -> 72.8 us
    pallas_call x0 -> x1, Pallas kernels: none -> 4.94 us  [local(): pl.pallas_call(finish, out_shape=(jax.ShapeDtypeStruct((tok_rows, feat),...]
    unnamed x7 -> x6, local copies, waits for them, and re-layouts: 5.04 us -> 3.17 us
    reshape x1 -> x0, local copies, waits for them, and re-layouts: 1.41 us -> none  [local(): send_index.reshape(-1, 1, LANES)]
    squeeze x1 -> x0, local copies, waits for them, and re-layouts: 1.27 us -> none  [local(): return (point_grads, inner_total, outer_total, biases[0], biases[1])]
    pallas_call x1, Pallas kernels: 68.6 us -> 67.8 us  [local(): pl.pallas_call(functools.partial(kernel, sweeps, tiles, scaling), out_sha...]
where the time goes in v2:
time: 77.4 us; the launch traced here: 77.2 us
  Pallas kernels  72.8 us (94%)
  local copies, waits for them, and re-layouts  3.17 us (4%)
  between operations  1.3 us (2%)
    pallas_call x1, Pallas kernels, local(): pl.pallas_call(functools.partial(kernel, sweeps, tiles, scaling), out_sha...  67.8 us
    pallas_call x1, Pallas kernels, local(): pl.pallas_call(finish, out_shape=(jax.ShapeDtypeStruct((tok_rows, feat),...  4.94 us
    unnamed x6, local copies, waits for them, and re-layouts  3.17 us

profile of v2, /device:TPU:0, one launch (start us, length us, event | category | flops | bytes accessed | tf_op | source)
XLA Modules:
  0.0 77.2 jit_solution(16222931318026568037)
XLA Ops:
  1.3 67.8 %exchange.1 = (bf16[16384,128]{1,0:T(8,128)(2,1)S(1)}, f32[16,16,128]{2,1,0:T(8,128)S(1)}, f32[2,128]{1,0:T(2,128)S(1)}) custom-call(s32[1]{0:T(128)S(6)} %copy.14.live_ref, bf16[9216,128]{1,0:T(8,128)(2,1)} %cot_ref.1, s32[1,16,512]{2,1,0:T(8,128)} %send_ref.1, s32[128,1,128]{2,1,0:T(1,128)} %bitcast.3, bf16[128,128]{1,0:T(8,128)(2,1)} %inner_w_ref.1, ...), custom_call_target="tpu_custom_call" | custom-call | flops 4294967296 | bytes 12582912 | tf_op jit(solution)/shard_map/exchange/pallas_call | solution.py:330
  69.1 0.0 copy-start
  69.1 1.9 %copy-done = bf16[16384,128]{1,0:T(8,128)(2,1)} copy-done((bf16[16384,128]{1,0:T(8,128)(2,1)}, bf16[16384,128]{1,0:T(8,128)(2,1)S(1)}, u32[]{:S(2)}) %copy-start) | copy-done | bytes 4194328
  71.1 0.0 copy-start.1
  71.1 0.6 copy-done.1
  71.7 0.0 copy-start.2
  71.7 0.6 copy-done.2
  72.3 4.9 %finish.1 = (bf16[16384,128]{1,0:T(8,128)(2,1)}, f32[128,128]{1,0:T(8,128)}, f32[128,128]{1,0:T(8,128)}, f32[128]{0:T(128)}, f32[128]{0:T(128)}) custom-call(bf16[16384,128]{1,0:T(8,128)(2,1)} %copy-done, f32[16,16,128]{2,1,0:T(8,128)} %copy-done.1, f32[2,128]{1,0:T(2,128)} %copy-done.2), custom_call_target="tpu_custom_call" | custom-call | tf_op jit(solution)/shard_map/finish/pallas_call | solution.py:380
Async XLA Ops:
  69.1 1.9 %copy-start = (bf16[16384,128]{1,0:T(8,128)(2,1)}, bf16[16384,128]{1,0:T(8,128)(2,1)S(1)}, u32[]{:S(2)}) copy-start(bf16[16384,128]{1,0:T(8,128)(2,1)S(1)} %get-tuple-element.8.grads_in) | copy-start | bytes 12582916
  71.1 0.6 copy-start.1
  71.7 0.6 copy-start.2

commit v3 on v2

--- a/solution.py
+++ b/solution.py
@@ -34,18 +34,19 @@
     tiles,
     scaling,
     live_ref,
-    cot_ref,
     send_ref,
     slot_ref,
     inner_w_ref,
     inner_b_ref,
     outer_w_ref,
     outer_b_ref,
+    cot_hbm,
     feats_hbm,
     grads,
     totals,
     bias_out,
     feats,
+    cot_ref,
     outgoing,
     received,
     act_ref,
@@ -63,6 +64,7 @@
     bias_slots,
     index_rows,
     feats_sem,
+    cells_sem,
     row_send,
     row_recv,
     term_send,
@@ -85,7 +87,15 @@
     feat = feats.shape[1]
     me = lax.axis_index("sweep") * tiles + lax.axis_index("tile")
 
+    flips = [(1 - 2 * ((me // (1 << bit)) % 2)) * (1 << bit) for bit in range(bits)]
+
     def paired(base, step):
+        if isinstance(step, int):
+            shift = bits - (units.bit_length() - 1) if base is not me else 0
+            for bit in range(bits):
+                if (step >> bit) & 1:
+                    base = base + flips[bit + shift] // (1 << shift)
+            return base
         other = 0
         for bit in range(bits):
             scale = 1 << bit
@@ -98,21 +108,20 @@
     def far_near(turn):
         return (units - 1) - turn // 2 - (turn % 2) * (units // 2)
 
+    cells_load = pltpu.make_async_copy(cot_hbm, cot_ref, cells_sem)
+    cells_load.start()
     load = pltpu.make_async_copy(feats_hbm, feats, feats_sem)
     load.start()
 
     barrier = pltpu.get_barrier_semaphore()
 
-    def greet(step, carry):
+    for step in range(1, owners):
         pl.semaphore_signal(
             barrier,
             inc=1,
             device_id=device(paired(me, step)),
             device_id_type=pl.DeviceIdType.MESH,
         )
-        return carry
-
-    lax.fori_loop(1, owners, greet, 0)
 
     for peer in range(owners):
         for low in range(0, per_peer, LANES):
@@ -147,15 +156,17 @@
 
     def send_unit(turn, carry):
         unit_step = far_near(turn)
-        select(paired(my_unit, unit_step), outgoing)
         for sub in range(unit_peers):
             step = unit_step * unit_peers + sub
             row_copy(step, paired(me, step)).start()
+        unit_step = (far_near(turn + 1) + units) % units
+        select(paired(my_unit, unit_step), outgoing)
         return carry
 
+    cells_load.wait()
+    select(paired(my_unit, units - 1 + 0 * me), outgoing)
     pl.semaphore_wait(barrier, owners - 1)
     lax.fori_loop(0, units - 1, send_unit, 0)
-    select(my_unit, outgoing)
     own = pl.ds(pl.multiple_of(me * per_peer, per_peer), per_peer)
     received[own, :] = outgoing[own, :]
     for sub in range(1, unit_peers):
@@ -265,19 +276,16 @@
             device_id_type=pl.DeviceIdType.MESH,
         )
 
-    def each(act, first=1, last=None):
-        def body(turn, carry):
-            act(owners - turn)
-            return carry
-
-        lax.fori_loop(first, owners, body, 0)
+    def each(act):
+        for step in range(owners - 1, 0, -1):
+            act(step)
 
     each(lambda step: term_copy(step).start())
     each(lambda step: bias_copy(step).start())
     term_slots[me] = terms[me]
     bias_slots[me] = bias_term[...]
     each(lambda step: term_copy(step).wait_recv())
-    totals[me] = jnp.sum(term_slots[...], axis=0) * scaling
+    totals[me] = (jnp.sum(term_slots[...], axis=0) * scaling).astype(totals.dtype)
     each(lambda step: total_copy(step).start())
     each(lambda step: bias_copy(step).wait_recv())
     bias_out[...] = jnp.sum(bias_slots[...], axis=0) * scaling
@@ -290,17 +298,46 @@
 
 
 def finish(
-    grads_in, totals_in, biases_in, grads_out, inner_out, outer_out, ibias_out, obias_out, sems
+    grads_in,
+    totals_in,
+    biases_in,
+    grads_out,
+    inner_out,
+    outer_out,
+    ibias_out,
+    obias_out,
+    inner_full,
+    outer_full,
+    ibias_full,
+    obias_full,
+    sems,
 ):
+    pieces = sems.shape[0] - 4
+    rows = grads_in.shape[0] // pieces
+    copies = []
+    for piece in range(pieces):
+        place = pl.ds(piece * rows, rows)
+        copies.append(
+            pltpu.make_async_copy(grads_in.at[place], grads_out.at[place], sems.at[piece])
+        )
+        copies[-1].start()
     inner_parts = inner_out.shape[0] // totals_in.shape[1]
-    outer_parts = totals_in.shape[0] - inner_parts
-    copy = pltpu.make_async_copy(grads_in, grads_out, sems.at[0])
-    copy.start()
-    inner_out[...] = totals_in[:inner_parts].reshape(inner_out.shape)
-    outer_out[...] = totals_in[inner_parts:].reshape(outer_out.shape)
-    ibias_out[...] = biases_in[0]
-    obias_out[...] = biases_in[1]
-    copy.wait()
+    totals = totals_in[...].astype(jnp.float32)
+    inner_full[...] = totals[:inner_parts].reshape(inner_out.shape)
+    outer_full[...] = totals[inner_parts:].reshape(outer_out.shape)
+    ibias_full[...] = biases_in[0]
+    obias_full[...] = biases_in[1]
+    outputs = (
+        (inner_full, inner_out),
+        (outer_full, outer_out),
+        (ibias_full, ibias_out),
+        (obias_full, obias_out),
+    )
+    for place, (held, out) in enumerate(outputs):
+        copies.append(pltpu.make_async_copy(held, out, sems.at[pieces + place]))
+        copies[-1].start()
+    for copy in copies:
+        copy.wait()
 
 
 def local(
@@ -331,15 +368,16 @@
         functools.partial(kernel, sweeps, tiles, scaling),
         out_shape=(
             pltpu.VMEM((tok_rows, feat), half),
-            pltpu.VMEM((owners, share, LANES), full),
+            pltpu.VMEM((owners, share, LANES), half),
             pltpu.VMEM((2, width), full),
         ),
         in_specs=[pl.BlockSpec(memory_space=pltpu.SMEM)]
-        + [vmem] * 7
-        + [pl.BlockSpec(memory_space=pl.ANY)],
+        + [vmem] * 6
+        + [pl.BlockSpec(memory_space=pltpu.HBM)] * 2,
         out_specs=(vmem, vmem, vmem),
         scratch_shapes=[
             pltpu.VMEM((tok_rows, feat), half),
+            pltpu.VMEM(cotangent.shape, half),
             pltpu.VMEM((rows, channels), half),
             pltpu.VMEM((rows, channels), half),
             pltpu.VMEM((tok_rows, width), half),
@@ -357,10 +395,11 @@
             pltpu.VMEM((owners, 2, LANES), full),
             pltpu.VMEM((rows // LANES, 1, LANES), jnp.int32),
             dma(()),
+            dma(()),
         ]
         + [dma((owners,))] * 8,
         compiler_params=pltpu.CompilerParams(
-            collective_id=0, has_side_effects=True, vmem_limit_bytes=56 * 1024 * 1024
+            collective_id=0, has_side_effects=True, vmem_limit_bytes=57 * 1024 * 1024
         ),
         cost_estimate=pl.CostEstimate(
             flops=flops, bytes_accessed=12 * 1024 * 1024, transcendentals=2 * tok_rows * LANES
@@ -368,13 +407,13 @@
         name="exchange",
     )(
         live_count,
-        cotangent,
         send_index,
         point_slot.reshape(-1, 1, LANES),
         inner_weight,
         inner_bias.reshape(1, -1),
         outer_weight,
         outer_bias.reshape(1, -1),
+        cotangent,
         point_feats,
     )
     return pl.pallas_call(
@@ -387,10 +426,17 @@
             jax.ShapeDtypeStruct((channels,), full),
         ),
         in_specs=[vmem, vmem, vmem],
-        out_specs=(pl.BlockSpec(memory_space=pl.ANY), vmem, vmem, vmem, vmem),
-        scratch_shapes=[dma((1,))],
+        out_specs=[pl.BlockSpec(memory_space=pl.ANY)] * 5,
+        scratch_shapes=[
+            pltpu.VMEM((feat, width), full),
+            pltpu.VMEM((width, channels), full),
+            pltpu.VMEM((width,), full),
+            pltpu.VMEM((channels,), full),
+            dma((8,)),
+        ],
+        compiler_params=pltpu.CompilerParams(vmem_limit_bytes=4 * 1024 * 1024),
         name="finish",
-    )(grads, totals, biases)
+    )(*(pltpu.with_memory_space_constraint(x, pltpu.VMEM) for x in (grads, totals, biases)))
 
 
 def solution(mesh):

time: 77.4 us -> 68.9 us (0.89)
  Pallas kernels: 72.8 us -> 67.5 us
  local copies, waits for them, and re-layouts: 3.17 us -> 0 us
    unnamed x6 -> x0, local copies, waits for them, and re-layouts: 3.17 us -> none
    pallas_call x1, Pallas kernels: 4.94 us -> 2.11 us  [local(): pl.pallas_call(finish, out_shape=(jax.ShapeDtypeStruct((tok_rows, feat),...]
    pallas_call x1, Pallas kernels: 67.8 us -> 65.3 us  [local(): pl.pallas_call(functools.partial(kernel, sweeps, tiles, scaling), out_sha...]
where the time goes in v3:
time: 68.9 us; the launch traced here: 68.7 us
  Pallas kernels  67.5 us (98%)
  between operations  1.29 us (2%)
    pallas_call x1, Pallas kernels, local(): pl.pallas_call(functools.partial(kernel, sweeps, tiles, scaling), out_sha...  65.3 us
    pallas_call x1, Pallas kernels, local(): pl.pallas_call(finish, out_shape=(jax.ShapeDtypeStruct((tok_rows, feat),...  2.11 us

profile of v3, /device:TPU:0, one launch (start us, length us, event | category | flops | bytes accessed | tf_op | source)
XLA Modules:
  0.0 68.7 jit_solution(11364976005724425351)
XLA Ops:
  1.3 65.3 %exchange.1 = (bf16[16384,128]{1,0:T(8,128)(2,1)S(1)}, bf16[16,16,128]{2,1,0:T(8,128)(2,1)S(1)}, f32[2,128]{1,0:T(2,128)S(1)}) custom-call(s32[1]{0:T(128)S(6)} %copy.14.live_ref, s32[1,16,512]{2,1,0:T(8,128)} %send_ref.1, s32[128,1,128]{2,1,0:T(1,128)} %bitcast.3, bf16[128,128]{1,0:T(8,128)(2,1)} %inner_w_ref.1, f32[1,128]{1,0:T(1,128)} %bitcast.4, ...), custom_call_target="tpu_custom_call" | custom-call | flops 4294967296 | bytes 12582912 | tf_op jit(solution)/shard_map/exchange/pallas_call | solution.py:367
  66.6 2.1 %finish.1 = (bf16[16384,128]{1,0:T(8,128)(2,1)}, f32[128,128]{1,0:T(8,128)}, f32[128,128]{1,0:T(8,128)}, f32[128]{0:T(128)}, f32[128]{0:T(128)}) custom-call(bf16[16384,128]{1,0:T(8,128)(2,1)S(1)} %get-tuple-element.8.grads_in, bf16[16,16,128]{2,1,0:T(8,128)(2,1)S(1)} %get-tuple-element.9.totals_in, f32[2,128]{1,0:T(2,128)S(1)} %get-tuple-element.10.biases_in), custom_call_target="tpu_custom_call" | custom-call | tf_op jit(solution)/shard_map/finish/pallas_call | solution.py:419

commit v4 on v3

--- a/solution.py
+++ b/solution.py
@@ -35,11 +35,11 @@
     scaling,
     live_ref,
     send_ref,
-    slot_ref,
-    inner_w_ref,
-    inner_b_ref,
-    outer_w_ref,
-    outer_b_ref,
+    slot_hbm,
+    inner_w_hbm,
+    inner_b_hbm,
+    outer_w_hbm,
+    outer_b_hbm,
     cot_hbm,
     feats_hbm,
     grads,
@@ -63,6 +63,12 @@
     bias_term,
     bias_slots,
     index_rows,
+    slot_ref,
+    inner_w_ref,
+    inner_b_ref,
+    outer_w_ref,
+    outer_b_ref,
+    side_sems,
     feats_sem,
     cells_sem,
     row_send,
@@ -111,7 +117,19 @@
     cells_load = pltpu.make_async_copy(cot_hbm, cot_ref, cells_sem)
     cells_load.start()
     load = pltpu.make_async_copy(feats_hbm, feats, feats_sem)
-    load.start()
+
+    side_loads = [
+        pltpu.make_async_copy(source, target, side_sems.at[place])
+        for place, (source, target) in enumerate(
+            (
+                (slot_hbm, slot_ref),
+                (inner_w_hbm, inner_w_ref),
+                (inner_b_hbm, inner_b_ref),
+                (outer_w_hbm, outer_w_ref),
+                (outer_b_hbm, outer_b_ref),
+            )
+        )
+    ]
 
     barrier = pltpu.get_barrier_semaphore()
 
@@ -164,6 +182,9 @@
         return carry
 
     cells_load.wait()
+    load.start()
+    for side in side_loads:
+        side.start()
     select(paired(my_unit, units - 1 + 0 * me), outgoing)
     pl.semaphore_wait(barrier, owners - 1)
     lax.fori_loop(0, units - 1, send_unit, 0)
@@ -172,6 +193,8 @@
     for sub in range(1, unit_peers):
         row_copy(sub, paired(me, sub)).start()
 
+    for side in side_loads:
+        side.wait()
     inner_wt[...] = inner_w_ref[...].T
     outer_wt[...] = outer_w_ref[...].T
     inner_acc[...] = jnp.zeros_like(inner_acc)
@@ -372,8 +395,8 @@
             pltpu.VMEM((2, width), full),
         ),
         in_specs=[pl.BlockSpec(memory_space=pltpu.SMEM)]
-        + [vmem] * 6
-        + [pl.BlockSpec(memory_space=pltpu.HBM)] * 2,
+        + [vmem]
+        + [pl.BlockSpec(memory_space=pltpu.HBM)] * 7,
         out_specs=(vmem, vmem, vmem),
         scratch_shapes=[
             pltpu.VMEM((tok_rows, feat), half),
@@ -394,6 +417,12 @@
             pltpu.VMEM((2, LANES), full),
             pltpu.VMEM((owners, 2, LANES), full),
             pltpu.VMEM((rows // LANES, 1, LANES), jnp.int32),
+            pltpu.VMEM((tok_rows // LANES, 1, LANES), jnp.int32),
+            pltpu.VMEM((feat, width), half),
+            pltpu.VMEM((1, width), full),
+            pltpu.VMEM((width, channels), half),
+            pltpu.VMEM((1, channels), full),
+            dma((5,)),
             dma(()),
             dma(()),
         ]

time: 68.9 us -> 68.9 us (level)
  no operation moved by 1% of the time
where the time goes in v4:
time: 68.9 us; the launch traced here: 68.7 us
  Pallas kernels  67.4 us (98%)
  between operations  1.29 us (2%)
    pallas_call x1, Pallas kernels, local(): pl.pallas_call(functools.partial(kernel, sweeps, tiles, scaling), out_sha...  65.3 us
    pallas_call x1, Pallas kernels, local(): pl.pallas_call(finish, out_shape=(jax.ShapeDtypeStruct((tok_rows, feat),...  2.11 us

profile of v4, /device:TPU:0, one launch (start us, length us, event | category | flops | bytes accessed | tf_op | source)
XLA Modules:
  0.0 68.7 jit_solution(2943985197377017999)
XLA Ops:
  1.3 65.3 %exchange.1 = (bf16[16384,128]{1,0:T(8,128)(2,1)S(1)}, bf16[16,16,128]{2,1,0:T(8,128)(2,1)S(1)}, f32[2,128]{1,0:T(2,128)S(1)}) custom-call(s32[1]{0:T(128)S(6)} %copy.14.live_ref, s32[1,16,512]{2,1,0:T(8,128)} %send_ref.1, s32[128,1,128]{2,1,0:T(1,128)} %bitcast.3, bf16[128,128]{1,0:T(8,128)(2,1)} %inner_w_hbm.1, f32[1,128]{1,0:T(1,128)} %bitcast.4, ...), custom_call_target="tpu_custom_call" | custom-call | flops 4294967296 | bytes 12582912 | tf_op jit(solution)/shard_map/exchange/pallas_call | solution.py:390
  66.6 2.1 %finish.1 = (bf16[16384,128]{1,0:T(8,128)(2,1)}, f32[128,128]{1,0:T(8,128)}, f32[128,128]{1,0:T(8,128)}, f32[128]{0:T(128)}, f32[128]{0:T(128)}) custom-call(bf16[16384,128]{1,0:T(8,128)(2,1)S(1)} %get-tuple-element.8.grads_in, bf16[16,16,128]{2,1,0:T(8,128)(2,1)S(1)} %get-tuple-element.9.totals_in, f32[2,128]{1,0:T(2,128)S(1)} %get-tuple-element.10.biases_in), custom_call_target="tpu_custom_call" | custom-call | tf_op jit(solution)/shard_map/finish/pallas_call | solution.py:448
